TPU v7x, 512 devices: a whole 4x4x16 slice. The times are simulated.
512 devices in a mesh: rep: 32 (over z_hi, x, core), fsdp: 16 (over y, z_lo).
Axes of the slice: x: 4, y: 4, z: 16 (z_hi: 4, z_lo: 4; z = z_hi * 4 + z_lo), core: 2. Of those that a mesh axis runs over, the one named last changes fastest.
Arguments:
- acts: bfloat16 [32, 3072, 512], P('rep', 'fsdp'), may hold values from -6 to 6
- cotangent: bfloat16 [32, 3072, 4096], P('rep', 'fsdp'), may hold values from -6 to 6
- weight: float32 [32, 512, 4096], P('rep', 'fsdp'), may hold values from -6 to 6
- moment_one: float32 [32, 512, 4096], P('rep', 'fsdp'), may hold values from -2 to 2
- moment_two: float32 [32, 512, 4096], P('rep', 'fsdp'), may hold values from 0.02 to 1
- learn_rate: float32 [1], replicated, may hold values from 0.05 to 0.3
- step_index: int32 [1], replicated, may hold values from 0 to 999
- step_count: int32 [1], replicated, may hold values from 1 to 19
Outputs:
- act_grad: bfloat16 [32, 3072, 512], P('rep', 'fsdp')
- new_weight: float32 [32, 512, 4096], P('rep', 'fsdp')
- new_moment_one: float32 [32, 512, 4096], P('rep', 'fsdp')
- new_moment_two: float32 [32, 512, 4096], P('rep', 'fsdp')
Inputs may be any that keep to these rules, and one draw needn't show every extreme that they name: `step_index`: the gossip step; the partner offset is 2 ** (t mod 4). `step_count`: the number of AdamW steps taken, this one included.
All inputs are finite; a program needn't handle non-finite values.
Results may differ from a plain program's by a relative error of at most 0.01.
Values may be sent and summed in bfloat16 or wider, within the bound.
A program may use at most 64 MiB of HBM per device.

v0:
```python
from functools import partial

import jax
import jax.numpy as jnp
from jax import lax
from jax.sharding import PartitionSpec as P

BETA_ONE = 0.9
BETA_TWO = 0.95
EPSILON = 1e-08
DECAY = 0.1
OUT_SCALE = 0.015625


def for_sending(value):
    return jax.tree.map(lambda a: a.astype(jnp.bfloat16) if a.dtype == jnp.float32 else a, value)


def shifted(block, axis, distance):
    devices = range(lax.axis_size(axis))
    route = [((i - distance) % len(devices), i) for i in devices]
    return lax.ppermute(block, axis, route)


def adamw_update(weight_in, moment_a, moment_b, gradient, learn_value, count_value):
    moment_a_up = BETA_ONE * moment_a + (1.0 - BETA_ONE) * gradient
    moment_b_up = BETA_TWO * moment_b + (1.0 - BETA_TWO) * gradient * gradient
    steps_float = count_value.astype(jnp.float32)
    fix_one = 1.0 - jnp.power(jnp.float32(BETA_ONE), steps_float)
    fix_two = 1.0 - jnp.power(jnp.float32(BETA_TWO), steps_float)
    direction = (
        moment_a_up / fix_one / (jnp.sqrt(moment_b_up / fix_two) + EPSILON) + DECAY * weight_in
    )
    return (weight_in - learn_value * direction, moment_a_up, moment_b_up)


def send_new(by_offset, values):
    return jax.tree.map(
        lambda part, own: part.astype(own.dtype),
        shifted(for_sending(values), "rep", by_offset),
        values,
    )


def from_partner(sender, level_index, values):
    branches = [partial(sender, 1 << level) for level in range(4)]
    return lax.switch(level_index, branches, values)


def local(acts, cotangent, weight, moment_one, moment_two, learn_rate, step_index, step_count):
    acts_dev = acts[0]
    cotan_dev = cotangent[0]
    weight_dev = weight[0]
    learn_value = learn_rate[0]
    count_value = step_count[0]
    level_index = step_index[0] % 4
    weight_low = weight_dev.astype(jnp.bfloat16)
    weight_whole = lax.all_gather(weight_low, "fsdp", axis=0, tiled=True)
    product = lax.dot_general(
        cotan_dev, weight_whole, (((1,), (1,)), ((), ())), preferred_element_type=jnp.float32
    )
    act_grad = (OUT_SCALE * product).astype(jnp.bfloat16)
    term = lax.dot_general(
        acts_dev, cotan_dev, (((0,), (0,)), ((), ())), preferred_element_type=jnp.float32
    )
    gradient = lax.psum_scatter(
        (OUT_SCALE * term).astype(jnp.bfloat16), "fsdp", scatter_dimension=0, tiled=True
    ).astype(jnp.float32)
    weight_up, moment_a_up, moment_b_up = adamw_update(
        weight_dev, moment_one[0], moment_two[0], gradient, learn_value, count_value
    )
    own_stack = jnp.stack([weight_up, moment_a_up, moment_b_up])
    partner_stack = from_partner(send_new, level_index, own_stack)
    mixed = 0.5 * (own_stack + partner_stack)
    return (act_grad[None], mixed[0][None], mixed[1][None], mixed[2][None])


def solution(mesh):
    in_specs = (
        P("rep", "fsdp", None),
        P("rep", "fsdp", None),
        P("rep", "fsdp", None),
        P("rep", "fsdp", None),
        P("rep", "fsdp", None),
        P(),
        P(),
        P(),
    )
    out_specs = (
        P("rep", "fsdp", None),
        P("rep", "fsdp", None),
        P("rep", "fsdp", None),
        P("rep", "fsdp", None),
    )
    return jax.shard_map(local, mesh=mesh, in_specs=in_specs, out_specs=out_specs, check_vma=False)
```

profile of v0, /device:TPU:96, one launch (start us, length us, event | category | flops | bytes accessed | tf_op | source)
XLA Modules:
  0.0 314.1 jit_solution(13142809317954203297)
XLA Ops:
  7.2 0.0 copy-start
  7.2 0.0 all-gather.2.cloned.1.call-start
  7.2 1.9 bitcast_convert_fusion
  9.1 0.0 all-gather.2.cloned.1.call-update
  9.1 0.0 reduce-scatter.2.cloned.1.call-start
  9.2 4.2 %multiply_convert_fusion = bf16[512,4096]{1,0:T(8,128)(2,1)} fusion(bf16[1,192,4096]{2,1,0:T(8,128)(2,1)S(1)} %copy-done, bf16[1,192,512]{2,1,0:T(8,128)(2,1)} %param.12), kind=kOutput, calls=%fused_computation | convolution fusion | flops 809500672 | bytes 5963776 | tf_op jit(solution)/shard_map/dot_general | solution.py:63
  13.4 0.0 reduce-scatter.2.cloned.1.call-update
  15.5 0.0 copy-start.4
  15.5 0.0 copy-start.5
  15.5 0.0 copy-start.6
  15.5 101.7 %all-gather.2.cloned.1.call-done = bf16[512,4096]{1,0:T(8,128)(2,1)} async-done(((bf16[32,4096]{1,0:T(8,128)(2,1)}), bf16[512,4096]{1,0:T(8,128)(2,1)}) %all-gather.2.cloned.1.call-update) | async-done | bytes 4194320 | tf_op jit(solution)/shard_map/all_gather | solution.py:58
  117.2 4.4 %fusion.9 = bf16[1,192,512]{2,1,0:T(8,128)(2,1)} fusion(bf16[512,4096]{1,0:T(8,128)(2,1)} %all-gather.2.cloned.1.call-done, bf16[1,192,4096]{2,1,0:T(8,128)(2,1)S(1)} %copy-done), kind=kOutput, calls=%fused_computation.8 | convolution fusion | flops 805502976 | bytes 5963776 | tf_op jit(solution)/shard_map/dot_general | solution.py:59
  121.6 102.9 %reduce-scatter.2.cloned.1.call-done = bf16[32,4096]{1,0:T(8,128)(2,1)} async-done(((bf16[512,4096]{1,0:T(8,128)(2,1)}), bf16[32,4096]{1,0:T(8,128)(2,1)}) %reduce-scatter.2.cloned.1.call-update) | async-done | bytes 262160 | tf_op jit(solution)/shard_map/reduce_scatter | solution.py:66
  224.5 1.4 fusion.16
  225.9 0.1 pad_maximum_fusion
  226.1 0.6 copy-done.1
  226.7 0.2 copy-done.2
  226.9 0.2 copy-done.3
  227.0 77.5 %conditional.4 = (f32[3,32,4096]{2,1,0:T(8,128)S(1)}) conditional(s32[]{:T(128)} %clamp.3, bf16[3,32,4096]{2,1,0:T(8,128)(2,1)S(1)} %pad_maximum_fusion, bf16[3,32,4096]{2,1,0:T(8,128)(2,1)S(1)} %pad_maximum_fusion, bf16[3,32,4096]{2,1,0:T(8,128)(2,1)S(1)} %pad_maximum_fusion, ...), branch_computations={%region_1.2_spmd, %region_2.3_spmd, %region_3.4_spmd, %region_4.5_... | conditional | flops 393216 | bytes 5505072
  227.0 3.4 %collective-permute-start.1 = (bf16[3,32,4096]{2,1,0:T(8,128)(2,1)S(1)}, bf16[3,32,4096]{2,1,0:T(8,128)(2,1)S(1)}, u32[]{:S(2)}, u32[]{:S(2)}) collective-permute-start(bf16[3,32,4096]{2,1,0:T(8,128)(2,1)S(1)} %param.1), channel_id=1, source_target_pairs={{480,0},{496,16},{0,32},{16,48},{32,64},{48,80},{64,96},{80,112},{... | collective-permute-start | bytes 2359304 | tf_op jit(solution)/shard_map/cond/branch_1_fun/ppermute | solution.py:22
  230.4 74.0 %collective-permute-done.1 = bf16[3,32,4096]{2,1,0:T(8,128)(2,1)S(1)} collective-permute-done((bf16[3,32,4096]{2,1,0:T(8,128)(2,1)S(1)}, bf16[3,32,4096]{2,1,0:T(8,128)(2,1)S(1)}, u32[]{:S(2)}, u32[]{:S(2)}) %collective-permute-start.1) | collective-permute-done | bytes 786464 | tf_op jit(solution)/shard_map/cond/branch_1_fun/ppermute | solution.py:22
  304.4 0.1 convert_element_type.40
  304.6 1.5 add_multiply_fusion
  306.1 1.2 fusion.20
  (7 shorter events, 0.0 us)
Async XLA Ops:
  7.2 2.0 copy-start
  7.2 110.0 %all-gather.2.cloned.1.call-start = ((), (), s32[]{:S(2)}) async-start(), calls=%async_computation.1 | async-start | bytes 4456448 | tf_op jit(solution)/shard_map/all_gather | solution.py:58
  9.1 215.4 %reduce-scatter.2.cloned.1.call-start = ((), (), s32[]{:S(2)}) async-start(), calls=%async_computation.2 | async-start | bytes 4456448 | tf_op jit(solution)/shard_map/reduce_scatter | solution.py:66
  15.5 209.1 %copy-start.4 = (f32[1,32,4096]{2,1,0:T(8,128)S(1)}, f32[1,32,4096]{2,1,0:T(8,128)}, u32[]{:S(2)}) copy-start(f32[1,32,4096]{2,1,0:T(8,128)} %param.14) | copy-start | bytes 1572868
  15.5 209.0 %copy-start.5 = (f32[1,32,4096]{2,1,0:T(8,128)S(1)}, f32[1,32,4096]{2,1,0:T(8,128)}, u32[]{:S(2)}) copy-start(f32[1,32,4096]{2,1,0:T(8,128)} %param.15) | copy-start | bytes 1572868
  15.5 209.0 %copy-start.6 = (f32[1,32,4096]{2,1,0:T(8,128)S(1)}, f32[1,32,4096]{2,1,0:T(8,128)}, u32[]{:S(2)}) copy-start(f32[1,32,4096]{2,1,0:T(8,128)} %param.16) | copy-start | bytes 1572868
  225.9 0.8 copy-start.1
  225.9 1.0 copy-start.2
  225.9 1.1 copy-start.3
  227.0 77.4 %collective-permute-start.1 = (bf16[3,32,4096]{2,1,0:T(8,128)(2,1)S(1)}, bf16[3,32,4096]{2,1,0:T(8,128)(2,1)S(1)}, u32[]{:S(2)}, u32[]{:S(2)}) collective-permute-start(bf16[3,32,4096]{2,1,0:T(8,128)(2,1)S(1)} %param.1), channel_id=1, source_target_pairs={{480,0},{496,16},{0,32},{16,48},{32,64},{48,80},{64,96},{80,112},{... | collective-permute-start | bytes 2359304 | tf_op jit(solution)/shard_map/cond/branch_1_fun/ppermute | solution.py:22
Sparse Core Ops, SparseCore 0:
  10.7 106.4 all-gather.1
  120.0 104.4 reduce-scatter.1
where the time goes:
time: 314 us
  waiting for transfers between devices  279 us (89%)
  between operations  16.2 us (5%)
  matrix products  8.6 us (3%)
  other arithmetic  5.05 us (2%)
  starting transfers between devices  3.45 us (1%)
    reduce_scatter x1, waiting for transfers between devices, local(): lax.psum_scatter((OUT_SCALE * term).astype(jnp.bfloat16), 'fsdp', scatter...  103 us
    all_gather x1, waiting for transfers between devices, local(): weight_whole = lax.all_gather(weight_low, 'fsdp', axis=0, tiled=True)  102 us
    ppermute x1, waiting for transfers between devices, shifted(): return lax.ppermute(block, axis, route)  74 us
  transfers between devices with their start and end apart: 3, of which 3 were waited for; matrix products, arithmetic and copies ran while one was open for 3% of the time, Pallas kernels for 0%

commit v1 on v0

v1 whole, which is shorter than its diff:
```python
from functools import partial

import jax
import jax.numpy as jnp
from jax import lax
from jax.experimental import pallas as pl
from jax.experimental.pallas import tpu as pltpu
from jax.sharding import PartitionSpec as P

BETA_ONE = 0.9
BETA_TWO = 0.95
EPSILON = 1e-08
DECAY = 0.1
OUT_SCALE = 0.015625

MESH = pl.DeviceIdType.MESH
F32 = jnp.float32
BF16 = jnp.bfloat16

N_Y = 4
N_Z = 4
TOK = 192
ROWS = 512
OWN = 32
D = 4096
SLICE = D // N_Y
CHUNKS = 4
CW = SLICE // CHUNKS

CROSSING = {1: ((3, 1),), 2: ((3, None),), 4: ((2, None), (3, None))}


def xor(index, bits):
    low = lax.rem(index, 2)
    high = lax.div(index, 2)
    if bits & 1:
        low = 1 - low
    if bits & 2:
        high = 1 - high
    return high * 2 + low


def gossip_kernel(
    offset,
    par_ref,
    acts_ref,
    cot_ref,
    w_ref,
    ma_ref,
    mb_ref,
    ag_out,
    w_out,
    ma_out,
    mb_out,
    w_low,
    w_full,
    acts_in,
    acts_t,
    cot_in,
    g_send,
    rs_in,
    gb_send,
    gb_in,
    ag_send,
    ag_in,
    go_send,
    go_in,
    relay_in,
    s_w,
    r_w,
    s_acts,
    r_acts,
    s_cot,
    r_cot,
    s_gz,
    r_gz,
    s_rs,
    r_rs,
    s_gb,
    r_gb,
    s_ag,
    r_ag,
    s_go,
    r_go,
    s_rel,
    r_rel,
    s_fwd,
):
    rep = lax.axis_index("rep")
    fs = lax.axis_index("fsdp")
    zh = lax.div(rep, 8)
    xc = lax.rem(rep, 8)
    x = lax.div(xc, 2)
    core = lax.rem(rep, 2)
    y = lax.div(fs, N_Z)
    z = lax.rem(fs, N_Z)

    def at_y(value):
        return (rep, value * N_Z + z)

    def at_z(value):
        return (rep, y * N_Z + value)

    def remote(src, dst, send, recv, device):
        return pltpu.make_async_remote_copy(
            src_ref=src, dst_ref=dst, send_sem=send, recv_sem=recv, device_id=device, device_id_type=MESH
        )

    target = (lax.rem(rep + offset, 32), fs)
    source = (lax.rem(rep + 32 - offset, 32), fs)
    slots = []
    if offset == 8:
        z_all = zh * N_Z + z
        z_down = lax.rem(z_all + 10, 16)
        z_up = lax.rem(z_all + 6, 16)
        down = (lax.div(z_down, N_Z) * 8 + xc, y * N_Z + lax.rem(z_down, N_Z))
        up = (lax.div(z_up, N_Z) * 8 + xc, y * N_Z + lax.rem(z_up, N_Z))
    else:
        next_zh = lax.rem(zh + 1, 4)
        prev_zh = lax.rem(zh + 3, 4)
        for sx, sc in CROSSING[offset]:
            dx = ((sx * 2 + (sc or 0) + offset) % 8) // 2
            if sc is None:
                dc = core
                is_src = x == sx
                is_relay = x != sx
                is_dst = x == dx
                src_rep = zh * 8 + sx * 2 + core
            else:
                dc = 1 - sc
                is_src = jnp.logical_and(x == sx, core == sc)
                is_relay = jnp.logical_and(x != sx, core == dc)
                is_dst = jnp.logical_and(x == dx, core == dc)
                src_rep = zh * 8 + sx * 2 + sc
            slots.append(
                dict(
                    sx=sx,
                    is_src=is_src,
                    is_relay=is_relay,
                    is_dst=is_dst,
                    src=(src_rep, fs),
                    dst=(next_zh * 8 + dx * 2 + dc, fs),
                    relay=[(zh * 8 + q * 2 + dc, fs) for q in range(4)],
                    back=[(prev_zh * 8 + q * 2 + dc, fs) for q in range(4)],
                )
            )

    barrier = pltpu.get_barrier_semaphore()

    def greet(device):
        pl.semaphore_signal(barrier, inc=1, device_id=device, device_id_type=MESH)

    for d in (1, 2, 3):
        greet(at_y(xor(y, d)))
        greet(at_z(xor(z, d)))
    greet(source)
    expected = 7
    if offset == 8:
        greet(up)
        expected = 8
    for slot in slots:

        @pl.when(slot["is_relay"])
        def _():
            greet(slot["src"])

        @pl.when(slot["is_dst"])
        def _():
            for q in range(4):
                if q != slot["sx"]:
                    greet(slot["back"][q])

        expected = expected + slot["is_relay"].astype(jnp.int32) + 3 * slot["is_src"].astype(jnp.int32)

    w_low[...] = w_ref[...].astype(BF16)
    pl.semaphore_wait(barrier, expected)

    def own_columns(peer, start, width):
        return pl.ds(pl.multiple_of(peer * SLICE + start, 128), width)

    w_copies, acts_copies = [], []
    cot_copies = [[] for _ in range(CHUNKS)]
    for d in (1, 2, 3):
        peer = xor(y, d)
        w_copies.append(
            remote(
                w_low.at[:, own_columns(peer, 0, SLICE)], w_full.at[y, z], s_w.at[d - 1], r_w.at[d - 1], at_y(peer)
            )
        )
        acts_copies.append(
            remote(acts_ref, acts_in.at[d - 1], s_acts.at[d - 1], r_acts.at[d - 1], at_y(peer))
        )
        for c in range(CHUNKS):
            cot_copies[c].append(
                remote(
                    cot_ref.at[:, own_columns(peer, c * CW, CW)],
                    cot_in.at[c, d],
                    s_cot.at[c, d - 1],
                    r_cot.at[c, d - 1],
                    at_y(peer),
                )
            )
    for copy in w_copies + acts_copies + cot_copies[0]:
        copy.start()
    w_full[y, z] = w_low[:, own_columns(y, 0, SLICE)]
    for c in range(1, CHUNKS):
        for copy in cot_copies[c]:
            copy.start()
    acts_t[0] = acts_ref[...].T
    for c in range(CHUNKS):
        cot_in[c, 0] = cot_ref[:, own_columns(y, c * CW, CW)]

    left = at_z(lax.rem(z + 3, 4))
    right = at_z(lax.rem(z + 1, 4))

    def pass_right(step):
        block = w_full.at[:, lax.rem(z + 4 - step, 4)]
        return remote(block, block, s_gz.at[0, step], r_gz.at[0, step], right)

    def pass_left(step):
        block = w_full.at[:, lax.rem(z + step, 4)]
        return remote(block, block, s_gz.at[1, step], r_gz.at[1, step], left)

    def gather_step(step):
        if step > 0:

            @pl.when(z >= step)
            def _():
                pass_right(step - 1).wait_recv()

            @pl.when(z <= 3 - step)
            def _():
                pass_left(step - 1).wait_recv()

        if step < 3:

            @pl.when(jnp.logical_and(z >= step, z < 3))
            def _():
                pass_right(step).start()

            @pl.when(jnp.logical_and(z <= 3 - step, z > 0))
            def _():
                pass_left(step).start()

    for copy in w_copies:
        copy.wait_recv()
    gather_step(0)

    for d in (1, 2, 3):
        acts_copies[d - 1].wait_recv()
        acts_t[d] = acts_in[d - 1].T
    gather_step(1)
    gather_step(2)

    rs_copies = [
        [
            remote(
                g_send.at[c, :, xor(z, d)], rs_in.at[c, d - 1], s_rs.at[c, d - 1], r_rs.at[c, d - 1], at_z(xor(z, d))
            )
            for d in (1, 2, 3)
        ]
        for c in range(CHUNKS)
    ]

    def gradient_chunk(c):
        for copy in cot_copies[c]:
            copy.wait_recv()
        for part in range(N_Y):
            total = None
            for d in range(4):
                term = jnp.dot(
                    acts_t[d, pl.ds(part * 128, 128), :], cot_in[c, d], preferred_element_type=F32
                )
                total = term if total is None else total + term
            g_send[c, part] = (OUT_SCALE * total).astype(BF16).reshape(N_Z, OWN, CW)
        for copy in rs_copies[c]:
            copy.start()

    gb_copies = [
        [
            remote(gb_send.at[c, xor(y, d)], gb_in.at[c, y], s_gb.at[c, d - 1], r_gb.at[c, d - 1], at_y(xor(y, d)))
            for d in (1, 2, 3)
        ]
        for c in range(CHUNKS)
    ]

    def reduce_chunk(c):
        for copy in rs_copies[c]:
            copy.wait_recv()
        total = g_send[c, :, z].astype(F32)
        for d in (1, 2, 3):
            total = total + rs_in[c, d - 1].astype(F32)
        gb_send[c] = total.astype(BF16)
        for copy in gb_copies[c]:
            copy.start()
        gb_in[c, y] = gb_send[c, y]

    learn = par_ref[0]
    scale_one = par_ref[1]
    scale_two = par_ref[2]

    def direct(c, q):
        return remote(go_send.at[c, q], go_in.at[c, q], s_go.at[c, q], r_go.at[c, q], target)

    def to_relay(c, q, slot_at, device):
        return remote(
            go_send.at[c, q], relay_in.at[c, slot_at], s_go.at[c, q], r_rel.at[c, slot_at], device
        )

    def go_on(c, q, slot_at, device):
        return remote(
            relay_in.at[c, slot_at], go_in.at[c, q], s_fwd.at[c, slot_at], r_go.at[c, q], device
        )

    def update_chunk(c):
        for copy in gb_copies[c]:
            copy.wait_recv()
        for q in range(4):
            columns = pl.ds(q * SLICE + c * CW, CW)
            grad = gb_in[c, q].astype(F32)
            weight = w_ref[:, columns]
            a_up = BETA_ONE * ma_ref[:, columns] + (1.0 - BETA_ONE) * grad
            b_up = BETA_TWO * mb_ref[:, columns] + (1.0 - BETA_TWO) * grad * grad
            direction = a_up * scale_one / (jnp.sqrt(b_up * scale_two) + EPSILON) + DECAY * weight
            w_up = weight - learn * direction
            go_send[c, q, 0] = w_up.astype(BF16)
            go_send[c, q, 1] = a_up.astype(BF16)
            go_send[c, q, 2] = b_up.astype(BF16)
            w_out[:, columns] = 0.5 * w_up
            ma_out[:, columns] = 0.5 * a_up
            mb_out[:, columns] = 0.5 * b_up
            if offset == 8:
                if q < 3:
                    direct(c, q).start()
                else:
                    to_relay(c, q, 0, down).start()
            else:
                by_relay = None
                for slot_at, slot in enumerate(slots):
                    if q != slot["sx"]:

                        @pl.when(slot["is_src"])
                        def _():
                            to_relay(c, q, slot_at, slot["relay"][q]).start()

                        by_relay = (
                            slot["is_src"] if by_relay is None else jnp.logical_or(by_relay, slot["is_src"])
                        )
                if by_relay is None:
                    direct(c, q).start()
                else:

                    @pl.when(jnp.logical_not(by_relay))
                    def _():
                        direct(c, q).start()

    def relay_chunk(c):
        if offset == 8:
            to_relay(c, 3, 0, down).wait_recv()
            go_on(c, 3, 0, down).start()
        for slot_at, slot in enumerate(slots):

            @pl.when(slot["is_relay"])
            def _():
                to_relay(c, 0, slot_at, target).wait_recv()
                go_on(c, x, slot_at, slot["dst"]).start()

    def mix_chunk(c):
        for q in range(4):
            direct(c, q).wait_recv()
            columns = pl.ds(q * SLICE + c * CW, CW)
            w_out[:, columns] += 0.5 * go_in[c, q, 0].astype(F32)
            ma_out[:, columns] += 0.5 * go_in[c, q, 1].astype(F32)
            mb_out[:, columns] += 0.5 * go_in[c, q, 2].astype(F32)

    def product(d):
        total = None
        for c in range(CHUNKS):
            block = w_full[:, :, :, pl.ds(c * CW, CW)].reshape(ROWS, CW)
            term = lax.dot_general(
                cot_in[c, d], block, (((1,), (1,)), ((), ())), preferred_element_type=F32
            )
            total = term if total is None else total + term
        return total

    ag_copies = [
        remote(ag_send.at[d - 1], ag_in.at[d - 1], s_ag.at[d - 1], r_ag.at[d - 1], at_y(xor(y, d)))
        for d in (1, 2, 3)
    ]

    def act_grad_send():
        gather_step(3)
        for d in (2, 1, 3):
            ag_send[d - 1] = product(d).astype(BF16)
            ag_copies[d - 1].start()

    def act_grad_end():
        total = product(0)
        for d in (1, 2, 3):
            ag_copies[d - 1].wait_recv()
            total = total + ag_in[d - 1].astype(F32)
        ag_out[...] = (OUT_SCALE * total).astype(BF16)

    gradient_chunk(0)
    gradient_chunk(1)
    reduce_chunk(0)
    gradient_chunk(2)
    reduce_chunk(1)
    update_chunk(0)
    gradient_chunk(3)
    act_grad_send()
    reduce_chunk(2)
    update_chunk(1)
    relay_chunk(0)
    reduce_chunk(3)
    update_chunk(2)
    relay_chunk(1)
    update_chunk(3)
    relay_chunk(2)
    relay_chunk(3)
    mix_chunk(0)
    mix_chunk(1)
    act_grad_end()
    mix_chunk(2)
    mix_chunk(3)

    for copies in [w_copies, acts_copies, ag_copies] + cot_copies + rs_copies + gb_copies:
        for copy in copies:
            copy.wait_send()
    for step in range(3):

        @pl.when(jnp.logical_and(z >= step, z < 3))
        def _():
            pass_right(step).wait_send()

        @pl.when(jnp.logical_and(z <= 3 - step, z > 0))
        def _():
            pass_left(step).wait_send()

    for c in range(CHUNKS):
        for q in range(4):
            direct(c, q).wait_send()
        if offset == 8:
            go_on(c, 3, 0, down).wait_send()
        for slot_at, slot in enumerate(slots):

            @pl.when(slot["is_relay"])
            def _():
                go_on(c, 0, slot_at, slot["dst"]).wait_send()


def step_kernel(offset, collective):
    n_slots = len(CROSSING.get(offset, ((0, None),)))
    dma = pltpu.SemaphoreType.DMA
    vmem = pl.BlockSpec(memory_space=pltpu.VMEM)
    return pl.pallas_call(
        partial(gossip_kernel, offset),
        out_shape=(
            jax.ShapeDtypeStruct((TOK, ROWS), BF16),
            jax.ShapeDtypeStruct((OWN, D), F32),
            jax.ShapeDtypeStruct((OWN, D), F32),
            jax.ShapeDtypeStruct((OWN, D), F32),
        ),
        in_specs=[pl.BlockSpec(memory_space=pltpu.SMEM)] + [vmem] * 5,
        out_specs=(vmem,) * 4,
        scratch_shapes=[
            pltpu.VMEM((OWN, D), BF16),
            pltpu.VMEM((N_Y, N_Z, OWN, SLICE), BF16),
            pltpu.VMEM((3, TOK, ROWS), BF16),
            pltpu.VMEM((4, ROWS, TOK), BF16),
            pltpu.VMEM((CHUNKS, 4, TOK, CW), BF16),
            pltpu.VMEM((CHUNKS, N_Y, N_Z, OWN, CW), BF16),
            pltpu.VMEM((CHUNKS, 3, N_Y, OWN, CW), BF16),
            pltpu.VMEM((CHUNKS, N_Y, OWN, CW), BF16),
            pltpu.VMEM((CHUNKS, N_Y, OWN, CW), BF16),
            pltpu.VMEM((3, TOK, ROWS), BF16),
            pltpu.VMEM((3, TOK, ROWS), BF16),
            pltpu.VMEM((CHUNKS, 4, 3, OWN, CW), BF16),
            pltpu.VMEM((CHUNKS, 4, 3, OWN, CW), BF16),
            pltpu.VMEM((CHUNKS, n_slots, 3, OWN, CW), BF16),
            dma((3,)),
            dma((3,)),
            dma((3,)),
            dma((3,)),
            dma((CHUNKS, 3)),
            dma((CHUNKS, 3)),
            dma((2, 3)),
            dma((2, 3)),
            dma((CHUNKS, 3)),
            dma((CHUNKS, 3)),
            dma((CHUNKS, 3)),
            dma((CHUNKS, 3)),
            dma((3,)),
            dma((3,)),
            dma((CHUNKS, 4)),
            dma((CHUNKS, 4)),
            dma((CHUNKS, n_slots)),
            dma((CHUNKS, n_slots)),
            dma((CHUNKS, n_slots)),
        ],
        compiler_params=pltpu.CompilerParams(
            collective_id=collective, has_side_effects=True, vmem_limit_bytes=48 << 20
        ),
        name="gossip_step_%d" % offset,
    )


def local(acts, cotangent, weight, moment_one, moment_two, learn_rate, step_index, step_count):
    steps_float = step_count[0].astype(F32)
    fix_one = 1.0 - jnp.power(F32(BETA_ONE), steps_float)
    fix_two = 1.0 - jnp.power(F32(BETA_TWO), steps_float)
    numbers = jnp.stack([learn_rate[0], 1.0 / fix_one, 1.0 / fix_two])
    outs = lax.switch(
        step_index[0] % 4,
        [step_kernel(1 << level, level) for level in range(4)],
        numbers,
        acts[0],
        cotangent[0],
        weight[0],
        moment_one[0],
        moment_two[0],
    )
    return tuple(out[None] for out in outs)


def solution(mesh):
    split = P("rep", "fsdp", None)
    return jax.shard_map(
        local,
        mesh=mesh,
        in_specs=(split,) * 5 + (P(),) * 3,
        out_specs=(split,) * 4,
        check_vma=False,
    )
```

time: 314 us -> 100 us (0.32)
  waiting for transfers between devices: 279 us -> 0 us
  Pallas kernels: 0 us -> 93.6 us
  between operations: 16.2 us -> 2.76 us
  matrix products: 8.6 us -> 0 us
  other arithmetic: 5.05 us -> 0.08 us
  starting transfers between devices: 3.45 us -> 0 us
    reduce_scatter x1 -> x0, waiting for transfers between devices: 103 us -> none  [local(): lax.psum_scatter((OUT_SCALE * term).astype(jnp.bfloat16), 'fsdp', scatter...]
    all_gather x1 -> x0, waiting for transfers between devices: 102 us -> none  [local(): weight_whole = lax.all_gather(weight_low, 'fsdp', axis=0, tiled=True)]
    pallas_call x0 -> x1, Pallas kernels: none -> 93.6 us  [local(): lax.switch(step_index[0] % 4, [step_kernel(1 << level, level) for level i...]
    ppermute x1 -> x0, waiting for transfers between devices: 74 us -> none  [shifted(): return lax.ppermute(block, axis, route)]
    dot_general x2 -> x0, matrix products: 8.6 us -> none  [the longest x1 4.4 us: local(): lax.dot_general(cotan_dev, weight_whole, (((1,), (1,)), ((), ())), prefer...]
    ppermute x1 -> x0, starting transfers between devices: 3.36 us -> none  [shifted(): return lax.ppermute(block, axis, route)]
  transfers between devices with their start and end apart: 3 -> 0, of which waited for: 3 -> 0; matrix products, arithmetic and copies ran while one was open for 3% -> 0% of each run, Pallas kernels for 0% -> 0%
where the time goes in v1:
time: 100 us
  Pallas kernels  93.6 us (94%)
  local copies, waits for them, and re-layouts  3.06 us (3%)
  between operations  2.76 us (3%)
    pallas_call x1, Pallas kernels, local(): lax.switch(step_index[0] % 4, [step_kernel(1 << level, level) for level i...  93.6 us
    unnamed x4, local copies, waits for them, and re-layouts  3.06 us

profile of v1, /device:TPU:96, one launch (start us, length us, event | category | flops | bytes accessed | tf_op | source)
XLA Modules:
  0.0 100.0 jit_solution(15381641365543285715)
XLA Ops:
  2.7 0.1 pad_maximum_fusion
  2.8 94.1 %conditional.1 = ((bf16[192,512]{1,0:T(8,128)(2,1)S(1)}, f32[32,4096]{1,0:T(8,128)S(1)}, f32[32,4096]{1,0:T(8,128)S(1)}, f32[32,4096]{1,0:T(8,128)S(1)})) conditional(s32[]{:T(128)} %clamp.3, (bf16[1,192,512]{2,1,0:T(8,128)(2,1)}, bf16[1,192,4096]{2,1,0:T(8,128)(2,1)}, f32[1,32,4096]{2,1,0:T(8,128)}, ...), branch_computations={%region_0.1_spmd, %region_1.2_spmd, %region_2.3_spmd, %region_3.4_... | conditional | bytes 8 | solution.py:513
  2.8 93.6 %gossip_step_4.1 = (bf16[192,512]{1,0:T(8,128)(2,1)S(1)}, f32[32,4096]{1,0:T(8,128)S(1)}, f32[32,4096]{1,0:T(8,128)S(1)}, f32[32,4096]{1,0:T(8,128)S(1)}) custom-call(f32[3]{0:T(128)S(1)} %get-tuple-element.108.par_ref, bf16[192,512]{1,0:T(8,128)(2,1)} %bitcast.46, bf16[192,4096]{1,0:T(8,128)(2,1)} %bitcast.30, f32[32,4096]{1,0:T(8,128)} %bitcast.34, ...), custom_call_target="tpu_custom_call" | custom-call | tf_op jit(solution)/shard_map/cond/branch_2_fun/gossip_step_4/pallas_call | solution.py:513
  96.9 0.7 copy.35
  97.6 0.8 copy.36
  98.4 0.8 copy.37
  99.2 0.8 copy.38

commit v2 on v1

v2 whole, which is shorter than its diff:
```python
from functools import partial

import jax
import jax.numpy as jnp
from jax import lax
from jax.experimental import pallas as pl
from jax.experimental.pallas import tpu as pltpu
from jax.sharding import PartitionSpec as P

BETA_ONE = 0.9
BETA_TWO = 0.95
EPSILON = 1e-08
DECAY = 0.1
OUT_SCALE = 0.015625

MESH = pl.DeviceIdType.MESH
F32 = jnp.float32
BF16 = jnp.bfloat16

N_Y = 4
N_Z = 4
TOK = 192
ROWS = 512
OWN = 32
D = 4096
SLICE = D // N_Y
CHUNKS = 4
CW = SLICE // CHUNKS
HALF = SLICE // 2

STRAIGHT = 1
EARLY = {1: 1, 2: 1, 4: 1, 8: 1}

CROSSING = {1: ((3, 1),), 2: ((3, None),), 4: ((2, None), (3, None))}


def xor(index, bits):
    low = lax.rem(index, 2)
    high = lax.div(index, 2)
    if bits & 1:
        low = 1 - low
    if bits & 2:
        high = 1 - high
    return high * 2 + low


def gossip_kernel(
    offset,
    par_ref,
    acts_ref,
    cot_ref,
    w_hbm,
    ma_hbm,
    mb_hbm,
    ag_out,
    w_out,
    ma_out,
    mb_out,
    w_ref,
    ma_ref,
    mb_ref,
    w_low,
    w_full,
    acts_in,
    acts_t,
    cot_in,
    g_send,
    rs_in,
    total,
    gb_send,
    gb_in,
    ag_send,
    ag_in,
    ag_sum,
    go_send,
    go_in,
    relay_in,
    gg_in,
    relay_gg,
    s_w,
    r_w,
    s_acts,
    r_acts,
    s_cot,
    r_cot,
    s_gz,
    r_gz,
    s_rs,
    r_rs,
    s_gb,
    r_gb,
    s_ag,
    r_ag,
    s_go,
    r_go,
    r_rel,
    s_fwd,
    s_gg,
    r_gg,
    r_relg,
    s_fwdg,
    s_own,
):
    rep = lax.axis_index("rep")
    fs = lax.axis_index("fsdp")
    zh = lax.div(rep, 8)
    xc = lax.rem(rep, 8)
    x = lax.div(xc, 2)
    core = lax.rem(rep, 2)
    y = lax.div(fs, N_Z)
    z = lax.rem(fs, N_Z)

    def at_y(value):
        return (rep, value * N_Z + z)

    def at_z(value):
        return (rep, y * N_Z + value)

    def remote(src, dst, send, recv, device):
        return pltpu.make_async_remote_copy(
            src_ref=src, dst_ref=dst, send_sem=send, recv_sem=recv, device_id=device, device_id_type=MESH
        )

    target = (lax.rem(rep + offset, 32), fs)
    source = (lax.rem(rep + 32 - offset, 32), fs)
    slots = []
    if offset == 8:
        z_all = zh * N_Z + z
        z_down = lax.rem(z_all + 10, 16)
        z_up = lax.rem(z_all + 6, 16)
        down = (lax.div(z_down, N_Z) * 8 + xc, y * N_Z + lax.rem(z_down, N_Z))
        up = (lax.div(z_up, N_Z) * 8 + xc, y * N_Z + lax.rem(z_up, N_Z))
    else:
        next_zh = lax.rem(zh + 1, 4)
        prev_zh = lax.rem(zh + 3, 4)
        for sx, sc in CROSSING[offset]:
            dx = ((sx * 2 + (sc or 0) + offset) % 8) // 2
            if sc is None:
                dc = core
                is_src = x == sx
                is_relay = x != sx
                is_dst = x == dx
                src_rep = zh * 8 + sx * 2 + core
            else:
                dc = 1 - sc
                is_src = jnp.logical_and(x == sx, core == sc)
                is_relay = jnp.logical_and(x != sx, core == dc)
                is_dst = jnp.logical_and(x == dx, core == dc)
                src_rep = zh * 8 + sx * 2 + sc
            slots.append(
                dict(
                    sx=sx,
                    is_src=is_src,
                    is_relay=is_relay,
                    is_dst=is_dst,
                    src=(src_rep, fs),
                    dst=(next_zh * 8 + dx * 2 + dc, fs),
                    relay=[(zh * 8 + q * 2 + dc, fs) for q in range(4)],
                    back=[(prev_zh * 8 + q * 2 + dc, fs) for q in range(4)],
                )
            )

    barrier = pltpu.get_barrier_semaphore()

    def greet(device):
        pl.semaphore_signal(barrier, inc=1, device_id=device, device_id_type=MESH)

    for d in (1, 2, 3):
        greet(at_y(xor(y, d)))
    for d in (1, 2, 3):
        greet(at_z(xor(z, d)))
    greet(source)
    expected = 7
    if offset == 8:
        greet(up)
        expected = 8
    for slot in slots:

        @pl.when(slot["is_relay"])
        def _():
            greet(slot["src"])

        @pl.when(slot["is_dst"])
        def _():
            for q in range(4):
                if q != slot["sx"]:
                    greet(slot["back"][q])

        expected = expected + slot["is_relay"].astype(jnp.int32) + 3 * slot["is_src"].astype(jnp.int32)

    early = EARLY[offset]
    first_early = CHUNKS - early
    first_straight = CHUNKS - STRAIGHT

    def part(q, c):
        return pl.ds(q * SLICE + c * CW, CW)

    def chunk(c):
        return pl.ds(c * CW, CW)

    def tokens(d):
        return pl.ds(d * TOK, TOK)

    own_cot = cot_ref.at[:, pl.ds(pl.multiple_of(y * SLICE, 128), SLICE)]
    own_copies = [
        pltpu.make_async_copy(src, dst, s_own.at[i])
        for i, (src, dst) in enumerate(
            (
                (w_hbm, w_ref),
                (acts_ref, acts_in.at[tokens(0)]),
                (own_cot, cot_in.at[tokens(0)]),
                (ma_hbm, ma_ref),
                (mb_hbm, mb_ref),
            )
        )
    ]
    for copy in own_copies:
        copy.start()
    own_copies[0].wait()
    w_low[...] = w_ref[...].astype(BF16)
    pl.semaphore_wait(barrier, expected)

    def own_columns(peer, start, width):
        return pl.ds(pl.multiple_of(peer * SLICE + start, 128), width)

    w_copies, acts_copies = [[], []], []
    cot_copies = [[] for _ in range(CHUNKS)]
    for d in (1, 2, 3):
        peer = xor(y, d)
        for h in range(2):
            w_copies[h].append(
                remote(
                    w_low.at[:, own_columns(peer, h * HALF, HALF)],
                    w_full.at[h, y, z],
                    s_w.at[h, d - 1],
                    r_w.at[h, d - 1],
                    at_y(peer),
                )
            )
        acts_copies.append(
            remote(acts_ref, acts_in.at[tokens(d)], s_acts.at[d - 1], r_acts.at[d - 1], at_y(peer))
        )
        for c in range(CHUNKS):
            cot_copies[c].append(
                remote(
                    cot_ref.at[:, own_columns(peer, c * CW, CW)],
                    cot_in.at[tokens(d), chunk(c)],
                    s_cot.at[c, d - 1],
                    r_cot.at[c, d - 1],
                    at_y(peer),
                )
            )
    for copy in w_copies[0] + w_copies[1] + acts_copies:
        copy.start()
    for c in range(CHUNKS):
        for copy in cot_copies[c]:
            copy.start()

    def ends(kind, c, q):
        if kind == 0:
            return go_send.at[c, q], go_in.at[c, q], s_go.at[c, q], r_go.at[c, q]
        e = c - first_early
        return gb_in.at[c, q], gg_in.at[e, q], s_gg.at[e, q], r_gg.at[e, q]

    def middle(kind, c, slot_at):
        if kind == 0:
            return relay_in.at[c, slot_at], r_rel.at[c, slot_at], s_fwd.at[c, slot_at]
        e = c - first_early
        return relay_gg.at[e, slot_at], r_relg.at[e, slot_at], s_fwdg.at[e, slot_at]

    def direct(kind, c, q):
        src, dst, send, recv = ends(kind, c, q)
        return remote(src, dst, send, recv, target)

    def to_relay(kind, c, q, slot_at, device):
        src, _, send, _ = ends(kind, c, q)
        hold, recv, _ = middle(kind, c, slot_at)
        return remote(src, hold, send, recv, device)

    def go_on(kind, c, q, slot_at, device):
        _, dst, _, recv = ends(kind, c, q)
        hold, _, send = middle(kind, c, slot_at)
        return remote(hold, dst, send, recv, device)

    def gossip_send(kind, c, q):
        if offset == 8:
            if q < 3:
                direct(kind, c, q).start()
            else:
                to_relay(kind, c, q, 0, down).start()
            return
        by_relay = None
        for slot_at, slot in enumerate(slots):
            if q != slot["sx"]:

                @pl.when(slot["is_src"])
                def _():
                    to_relay(kind, c, q, slot_at, slot["relay"][q]).start()

                by_relay = slot["is_src"] if by_relay is None else jnp.logical_or(by_relay, slot["is_src"])
        if by_relay is None:
            direct(kind, c, q).start()
        else:

            @pl.when(jnp.logical_not(by_relay))
            def _():
                direct(kind, c, q).start()

    def relay_chunk(kind, c):
        if offset == 8:
            to_relay(kind, c, 3, 0, down).wait_recv()
            go_on(kind, c, 3, 0, down).start()
        for slot_at, slot in enumerate(slots):

            @pl.when(slot["is_relay"])
            def _():
                to_relay(kind, c, 0, slot_at, target).wait_recv()
                go_on(kind, c, x, slot_at, slot["dst"]).start()

    def gossip_end(kind, c):
        for q in range(4):
            direct(kind, c, q).wait_send()
        if offset == 8:
            go_on(kind, c, 3, 0, down).wait_send()
        for slot_at, slot in enumerate(slots):

            @pl.when(slot["is_relay"])
            def _():
                go_on(kind, c, 0, slot_at, slot["dst"]).wait_send()

    for h in range(2):
        w_full[h, y, z] = w_low[:, own_columns(y, h * HALF, HALF)]
    for copy in own_copies[1:]:
        copy.wait()
    for c in range(first_early, CHUNKS):
        for q in range(4):
            go_send[c, q, 0] = w_low[:, part(q, c)]
            go_send[c, q, 1] = ma_ref[:, part(q, c)].astype(BF16)
            go_send[c, q, 2] = mb_ref[:, part(q, c)].astype(BF16)
            gossip_send(0, c, q)

    left = at_z(lax.rem(z + 3, 4))
    right = at_z(lax.rem(z + 1, 4))

    def pass_right(h, step):
        block = w_full.at[h, :, lax.rem(z + 4 - step, 4)]
        return remote(block, block, s_gz.at[h, 0, step], r_gz.at[h, 0, step], right)

    def pass_left(h, step):
        block = w_full.at[h, :, lax.rem(z + step, 4)]
        return remote(block, block, s_gz.at[h, 1, step], r_gz.at[h, 1, step], left)

    def gather_step(h, step):
        if step == 0:
            for copy in w_copies[h]:
                copy.wait_recv()
        else:

            @pl.when(z >= step)
            def _():
                pass_right(h, step - 1).wait_recv()

            @pl.when(z <= 3 - step)
            def _():
                pass_left(h, step - 1).wait_recv()

        if step < 3:

            @pl.when(jnp.logical_and(z >= step, z < 3))
            def _():
                pass_right(h, step).start()

            @pl.when(jnp.logical_and(z <= 3 - step, z > 0))
            def _():
                pass_left(h, step).start()

    def activations():
        for copy in acts_copies:
            copy.wait_recv()
        acts_t[...] = acts_in[...].T

    def sum_right(c, t):
        return remote(g_send.at[c, :, t], rs_in.at[0, c, t], s_rs.at[0, c, t], r_rs.at[0, c, t], right)

    def sum_left(c, t):
        return remote(g_send.at[c, :, t], rs_in.at[1, c, t], s_rs.at[1, c, t], r_rs.at[1, c, t], left)

    def straight(c, d):
        peer = xor(z, d)
        return remote(g_send.at[c, :, peer], rs_in.at[0, c, d], s_rs.at[0, c, d], r_rs.at[0, c, d], at_z(peer))

    def add_and_pass(c, t, way):
        copy = (sum_right, sum_left)[way](c, t)
        copy.wait_recv()
        g_send[c, :, t] = (g_send[c, :, t].astype(F32) + rs_in[way, c, t].astype(F32)).astype(BF16)
        copy.start()

    def pass_one(c):
        @pl.when(z == 1)
        def _():
            add_and_pass(c, 3, 0)
            add_and_pass(c, 2, 0)

        @pl.when(z == 2)
        def _():
            add_and_pass(c, 0, 1)
            add_and_pass(c, 1, 1)

    def pass_two(c):
        @pl.when(z == 2)
        def _():
            add_and_pass(c, 3, 0)

        @pl.when(z == 1)
        def _():
            add_and_pass(c, 0, 1)

    def gradient_chunk(c):
        for copy in cot_copies[c]:
            copy.wait_recv()
        result = jnp.dot(acts_t[...], cot_in[:, chunk(c)], preferred_element_type=F32)
        g_send[c] = (OUT_SCALE * result).astype(BF16).reshape(N_Y, N_Z, OWN, CW)
        if c >= first_straight:
            for d in (2, 3, 1):
                straight(c, d).start()
        else:

            @pl.when(z == 0)
            def _():
                for t in (3, 2, 1):
                    sum_right(c, t).start()

            @pl.when(z == 3)
            def _():
                for t in (0, 1, 2):
                    sum_left(c, t).start()

    gb_copies = [
        [
            remote(gb_send.at[c, xor(y, d)], gb_in.at[c, y], s_gb.at[c, d - 1], r_gb.at[c, d - 1], at_y(xor(y, d)))
            for d in (1, 2, 3)
        ]
        for c in range(CHUNKS)
    ]

    def reduce_chunk(c):
        if c >= first_straight:
            result = g_send[c, :, z].astype(F32)
            for d in (1, 2, 3):
                straight(c, d).wait_recv()
                result = result + rs_in[0, c, d].astype(F32)
            gb_send[c] = result.astype(BF16)
        else:
            total[...] = g_send[c, :, z].astype(F32)

            @pl.when(z > 0)
            def _():
                sum_right(c, z).wait_recv()
                total[...] += rs_in[0, c, z].astype(F32)

            @pl.when(z < 3)
            def _():
                sum_left(c, z).wait_recv()
                total[...] += rs_in[1, c, z].astype(F32)

            gb_send[c] = total[...].astype(BF16)
        for copy in gb_copies[c]:
            copy.start()
        gb_in[c, y] = gb_send[c, y]

    learn = par_ref[0]
    scale_one = par_ref[1]
    scale_two = par_ref[2]

    def adamw(weight, moment_a, moment_b, grad):
        a_up = BETA_ONE * moment_a + (1.0 - BETA_ONE) * grad
        b_up = BETA_TWO * moment_b + (1.0 - BETA_TWO) * grad * grad
        direction = a_up * scale_one / (jnp.sqrt(b_up * scale_two) + EPSILON) + DECAY * weight
        return weight - learn * direction, a_up, b_up

    def update_chunk(c):
        for copy in gb_copies[c]:
            copy.wait_recv()
        if c >= first_early:
            for q in range(4):
                gossip_send(1, c, q)
        for q in range(4):
            columns = part(q, c)
            w_up, a_up, b_up = adamw(
                w_ref[:, columns], ma_ref[:, columns], mb_ref[:, columns], gb_in[c, q].astype(F32)
            )
            if c < first_early:
                go_send[c, q, 0] = w_up.astype(BF16)
                go_send[c, q, 1] = a_up.astype(BF16)
                go_send[c, q, 2] = b_up.astype(BF16)
                gossip_send(0, c, q)
            w_out[:, columns] = 0.5 * w_up
            ma_out[:, columns] = 0.5 * a_up
            mb_out[:, columns] = 0.5 * b_up

    def mix_chunk(c):
        for q in range(4):
            direct(0, c, q).wait_recv()
            columns = part(q, c)
            w_up, a_up, b_up = (go_in[c, q, k].astype(F32) for k in range(3))
            if c >= first_early:
                direct(1, c, q).wait_recv()
                w_up, a_up, b_up = adamw(w_up, a_up, b_up, gg_in[c - first_early, q].astype(F32))
            w_out[:, columns] += 0.5 * w_up
            ma_out[:, columns] += 0.5 * a_up
            mb_out[:, columns] += 0.5 * b_up

    def product(d, h):
        return lax.dot_general(
            cot_in[tokens(d), pl.ds(h * HALF, HALF)],
            w_full[h].reshape(ROWS, HALF),
            (((1,), (1,)), ((), ())),
            preferred_element_type=F32,
        )

    def act_grad_start(d):
        ag_sum[d] = product(d, 0)

    ag_copies = [
        remote(ag_send.at[d - 1], ag_in.at[d - 1], s_ag.at[d - 1], r_ag.at[d - 1], at_y(xor(y, d)))
        for d in (1, 2, 3)
    ]

    def act_grad_send(d):
        ag_send[d - 1] = (ag_sum[d] + product(d, 1)).astype(BF16)
        ag_copies[d - 1].start()

    def act_grad_end():
        result = ag_sum[0] + product(0, 1)
        for d in (1, 2, 3):
            ag_copies[d - 1].wait_recv()
            result = result + ag_in[d - 1].astype(F32)
        ag_out[...] = (OUT_SCALE * result).astype(BF16)

    steps = [
        (8.0, gather_step, 0, 0),
        (9.5, gather_step, 1, 0),
        (12.5, gather_step, 0, 1),
        (15.5, gather_step, 1, 1),
        (16.0, activations),
        (17.5, gather_step, 0, 2),
        (20.5, gather_step, 1, 2),
        (22.0, gather_step, 0, 3),
        (26.5, gather_step, 1, 3),
        (23.5, act_grad_start, 0),
        (24.0, act_grad_start, 2),
        (25.0, act_grad_start, 1),
        (26.0, act_grad_start, 3),
        (29.3, act_grad_send, 2),
        (30.0, act_grad_send, 1),
        (30.7, act_grad_send, 3),
        (42.0, act_grad_end),
    ]
    for c in range(CHUNKS):
        at = 17.0 + 12.0 / CHUNKS * (c + 1)
        steps.append((at, gradient_chunk, c))
        if c >= first_straight:
            at += 5.0
        else:
            steps.append((at + 3.0, pass_one, c))
            steps.append((at + 5.5, pass_two, c))
            at += 8.0
        steps.append((at, reduce_chunk, c))
        at += 2.5
        steps.append((at, update_chunk, c))
        if c >= first_early:
            steps.append((16.2, relay_chunk, 0, c))
            steps.append((at + 3.0, relay_chunk, 1, c))
        else:
            steps.append((at + 4.0, relay_chunk, 0, c))
        steps.append((at + 8.0, mix_chunk, c))
    for _, act, *with_args in sorted(steps, key=lambda step: step[0]):
        act(*with_args)

    for copies in w_copies + [acts_copies, ag_copies] + cot_copies + gb_copies:
        for copy in copies:
            copy.wait_send()
    for h in range(2):
        for step in range(3):

            @pl.when(jnp.logical_and(z >= step, z < 3))
            def _():
                pass_right(h, step).wait_send()

            @pl.when(jnp.logical_and(z <= 3 - step, z > 0))
            def _():
                pass_left(h, step).wait_send()

    for c in range(CHUNKS):
        if c >= first_straight:
            for d in (1, 2, 3):
                straight(c, d).wait_send()
        else:
            for t in range(N_Z):

                @pl.when(z < t)
                def _():
                    sum_right(c, t).wait_send()

                @pl.when(z > t)
                def _():
                    sum_left(c, t).wait_send()

        gossip_end(0, c)
        if c >= first_early:
            gossip_end(1, c)


def step_kernel(offset, collective):
    n_slots = len(CROSSING.get(offset, ((0, None),)))
    early = max(EARLY[offset], 1)
    dma = pltpu.SemaphoreType.DMA
    vmem = pl.BlockSpec(memory_space=pltpu.VMEM)
    return pl.pallas_call(
        partial(gossip_kernel, offset),
        out_shape=(
            jax.ShapeDtypeStruct((TOK, ROWS), BF16),
            jax.ShapeDtypeStruct((OWN, D), F32),
            jax.ShapeDtypeStruct((OWN, D), F32),
            jax.ShapeDtypeStruct((OWN, D), F32),
        ),
        in_specs=[pl.BlockSpec(memory_space=pltpu.SMEM)] + [pl.BlockSpec(memory_space=pltpu.HBM)] * 5,
        out_specs=(vmem,) * 4,
        scratch_shapes=[pltpu.VMEM((OWN, D), F32)] * 3
        + [
            pltpu.VMEM((OWN, D), BF16),
            pltpu.VMEM((2, N_Y, N_Z, OWN, HALF), BF16),
            pltpu.VMEM((4 * TOK, ROWS), BF16),
            pltpu.VMEM((ROWS, 4 * TOK), BF16),
            pltpu.VMEM((4 * TOK, SLICE), BF16),
            pltpu.VMEM((CHUNKS, N_Y, N_Z, OWN, CW), BF16),
            pltpu.VMEM((2, CHUNKS, N_Z, N_Y, OWN, CW), BF16),
            pltpu.VMEM((N_Y, OWN, CW), F32),
            pltpu.VMEM((CHUNKS, N_Y, OWN, CW), BF16),
            pltpu.VMEM((CHUNKS, N_Y, OWN, CW), BF16),
            pltpu.VMEM((3, TOK, ROWS), BF16),
            pltpu.VMEM((3, TOK, ROWS), BF16),
            pltpu.VMEM((4, TOK, ROWS), F32),
            pltpu.VMEM((CHUNKS, 4, 3, OWN, CW), BF16),
            pltpu.VMEM((CHUNKS, 4, 3, OWN, CW), BF16),
            pltpu.VMEM((CHUNKS, n_slots, 3, OWN, CW), BF16),
            pltpu.VMEM((early, 4, OWN, CW), BF16),
            pltpu.VMEM((early, n_slots, OWN, CW), BF16),
            dma((2, 3)),
            dma((2, 3)),
            dma((3,)),
            dma((3,)),
            dma((CHUNKS, 3)),
            dma((CHUNKS, 3)),
            dma((2, 2, 3)),
            dma((2, 2, 3)),
            dma((2, CHUNKS, N_Z)),
            dma((2, CHUNKS, N_Z)),
            dma((CHUNKS, 3)),
            dma((CHUNKS, 3)),
            dma((3,)),
            dma((3,)),
            dma((CHUNKS, 4)),
            dma((CHUNKS, 4)),
            dma((CHUNKS, n_slots)),
            dma((CHUNKS, n_slots)),
            dma((early, 4)),
            dma((early, 4)),
            dma((early, n_slots)),
            dma((early, n_slots)),
            dma((5,)),
        ],
        compiler_params=pltpu.CompilerParams(
            collective_id=collective, has_side_effects=True, vmem_limit_bytes=58 << 20
        ),
        name="gossip_step_%d" % offset,
    )


def local(acts, cotangent, weight, moment_one, moment_two, learn_rate, step_index, step_count):
    steps_float = step_count[0].astype(F32)
    fix_one = 1.0 - jnp.power(F32(BETA_ONE), steps_float)
    fix_two = 1.0 - jnp.power(F32(BETA_TWO), steps_float)
    numbers = jnp.stack([learn_rate[0], 1.0 / fix_one, 1.0 / fix_two])
    outs = lax.switch(
        step_index[0] % 4,
        [step_kernel(1 << level, level) for level in range(4)],
        numbers,
        acts[0],
        cotangent[0],
        weight[0],
        moment_one[0],
        moment_two[0],
    )
    return tuple(out[None] for out in outs)


def solution(mesh):
    split = P("rep", "fsdp", None)
    return jax.shard_map(
        local,
        mesh=mesh,
        in_specs=(split,) * 5 + (P(),) * 3,
        out_specs=(split,) * 4,
        check_vma=False,
    )
```

time: 100 us -> 97.5 us (0.975)
  the two profiles are of different devices: /device:TPU:96 before, /device:TPU:112 now
where the time goes in v2:
time: 97.5 us; the launch traced here: 97.3 us
  Pallas kernels  90.9 us (93%)
  local copies, waits for them, and re-layouts  3.06 us (3%)
  between operations  2.76 us (3%)
    pallas_call x1, Pallas kernels, local(): lax.switch(step_index[0] % 4, [step_kernel(1 << level, level) for level i...  90.9 us
    unnamed x4, local copies, waits for them, and re-layouts  3.06 us

profile of v2, /device:TPU:112, one launch (start us, length us, event | category | flops | bytes accessed | tf_op | source)
XLA Modules:
  0.0 97.3 jit_solution(3769118043257585251)
XLA Ops:
  2.7 0.1 pad_maximum_fusion
  2.8 91.4 %conditional.1 = ((bf16[192,512]{1,0:T(8,128)(2,1)S(1)}, f32[32,4096]{1,0:T(8,128)S(1)}, f32[32,4096]{1,0:T(8,128)S(1)}, f32[32,4096]{1,0:T(8,128)S(1)})) conditional(s32[]{:T(128)} %clamp.3, (bf16[1,192,512]{2,1,0:T(8,128)(2,1)}, bf16[1,192,4096]{2,1,0:T(8,128)(2,1)}, f32[1,32,4096]{2,1,0:T(8,128)}, ...), branch_computations={%region_0.1_spmd, %region_1.2_spmd, %region_2.3_spmd, %region_3.4_... | conditional | bytes 8 | solution.py:685
  2.8 90.9 %gossip_step_4.1 = (bf16[192,512]{1,0:T(8,128)(2,1)S(1)}, f32[32,4096]{1,0:T(8,128)S(1)}, f32[32,4096]{1,0:T(8,128)S(1)}, f32[32,4096]{1,0:T(8,128)S(1)}) custom-call(f32[3]{0:T(128)S(1)} %get-tuple-element.108.par_ref, bf16[192,512]{1,0:T(8,128)(2,1)} %bitcast.46, bf16[192,4096]{1,0:T(8,128)(2,1)} %bitcast.30, f32[32,4096]{1,0:T(8,128)} %bitcast.34, ...), custom_call_target="tpu_custom_call" | custom-call | tf_op jit(solution)/shard_map/cond/branch_2_fun/gossip_step_4/pallas_call | solution.py:685
  94.2 0.7 copy.35
  94.9 0.8 copy.36
  95.7 0.8 copy.37
  96.5 0.8 copy.38
